TPU v7x, 32 devices: a whole 2x2x4 slice. The times are simulated.
32 devices in a mesh: ctx: 2 (over y), tp: 16 (over z, x, core).
Axes of the slice: x: 2, y: 2, z: 4, core: 2. Of those that a mesh axis runs over, the one named last changes fastest.
Arguments:
- tokens: bfloat16 [1024, 4096], P(('ctx', 'tp')), may hold values from -6 to 6
- gate_weight: bfloat16 [4096, 16384], P(None, 'tp'), may hold values from -0.09375 to 0.09375
- input_weight: bfloat16 [4096, 16384], P(None, 'tp'), may hold values from -0.09375 to 0.09375
- state_weight: bfloat16 [4096, 2048], P(None, 'tp'), may hold values from -0.09375 to 0.09375
- step_weight: bfloat16 [4096, 256], P(None, 'tp'), may hold values from -0.09375 to 0.09375
- input_conv: float32 [5, 16384], P(None, 'tp'), may hold values from -0.5 to 0.5
- state_conv: float32 [5, 2048], P(None, 'tp'), may hold values from -0.5 to 0.5
- log_rate: float32 [256], P('tp'), may hold values from -12 to 2.1
- step_bias: float32 [256], P('tp'), may hold values from -6 to -2
- skip_gain: float32 [256], P('tp'), may hold values from 0.5 to 2
- norm_gain: float32 [16384], P('tp'), may hold values from 0.25 to 1.75
- out_weight: bfloat16 [16384, 4096], P('tp'), may hold values from -0.046875 to 0.046875
Outputs:
- mixed_out: bfloat16 [1024, 4096], P(('ctx', 'tp'))
All inputs are finite; a program needn't handle non-finite values.
Results may differ from a plain program's by a relative error of at most 0.0035.
The roundings to bfloat16 on the way count: a program that leaves them out, or rounds other values in their place, can miss the bound.
Values may be sent and summed in bfloat16 or wider, within the bound.
A program may use at most 128 MiB of HBM per device.

v0:
```python
import jax
import jax.numpy as jnp
from jax import lax
from jax.sharding import PartitionSpec as P

NSTATE = 256
GROUPS = 4
CONV = 4
SPAN = 64
DINNER = 16384


def passed_along(array, axis, by):
    peers = lax.axis_size(axis)
    pairs = [(i, i + by) for i in range(peers) if 0 <= i + by < peers]
    return lax.ppermute(array, axis, pairs)


def from_partner(array, axis, distance):
    return lax.ppermute(array, axis, [(i, i ^ 1 << distance) for i in range(lax.axis_size(axis))])


def prefix_2(part, axis, combine, identity):
    place = lax.axis_index(axis)
    gathered = jax.tree.map(lambda a: lax.all_gather(a, axis), part)
    state = jax.tree.map(lambda a, e: jnp.zeros_like(a) + jnp.asarray(e, a.dtype), part, identity)

    def one(hop, state):
        return combine(
            state, jax.tree.map(lambda a: lax.dynamic_index_in_dim(a, hop, 0, False), gathered)
        )

    return lax.fori_loop(0, place, one, state)


def span_terms(inputs, step_size, log_damp, write_vec, read_vec):
    highest = lax.Precision.HIGHEST
    cumulative = jnp.cumsum(log_damp, axis=1)
    length = log_damp.shape[1]
    causal = (jnp.arange(length)[:, None] >= jnp.arange(length)[None, :])[None, :, :, None]
    scores = jnp.einsum("kin,kjn->kij", read_vec, write_vec, precision=highest)
    spread = cumulative[:, :, None, :] - cumulative[:, None, :, :]
    damping = jnp.exp(jnp.where(causal, spread, -jnp.inf))
    mixing = scores[:, :, :, None] * damping * step_size[:, None, :, :]
    within = jnp.einsum("kijh,kjhp->kihp", mixing, inputs, precision=highest)
    to_end = jnp.exp(cumulative[:, -1:, :] - cumulative) * step_size
    states = jnp.einsum("kjh,kjhp,kjn->khpn", to_end, inputs, write_vec, precision=highest)
    return (cumulative, within, states)


def span_pass(cumulative, states, read_vec, zero_state):

    def advance(carried, payload):
        factor, increment = payload
        return (factor[:, None, None] * carried + increment, carried)

    last_state, entering = lax.scan(advance, zero_state, (jnp.exp(cumulative[:, -1, :]), states))
    across = jnp.einsum(
        "kih,kin,khpn->kihp",
        jnp.exp(cumulative),
        read_vec,
        entering,
        precision=lax.Precision.HIGHEST,
    )
    return (last_state, across)


def body(
    tokens,
    gate_weight,
    input_weight,
    state_weight,
    step_weight,
    input_conv,
    state_conv,
    log_rate,
    step_bias,
    skip_gain,
    norm_gain,
    out_weight,
):
    tensor_size = lax.axis_size("tp")
    per_group = tensor_size // GROUPS
    level_count = per_group.bit_length() - 1
    my_index = lax.axis_index("tp")
    local_width = gate_weight.shape[1]
    state_width = state_weight.shape[1]
    heads_here = log_rate.shape[0]
    head_dim = local_width // heads_here
    combined = jnp.concatenate([gate_weight, input_weight, state_weight, step_weight], axis=1)
    projected = jnp.dot(
        lax.all_gather(tokens, "tp", axis=0, tiled=True),
        combined,
        preferred_element_type=jnp.float32,
    )
    row_count = projected.shape[0]
    gate_rows = projected[:, :local_width].astype(jnp.bfloat16)
    streams = projected[:, local_width : 2 * local_width + state_width].astype(jnp.bfloat16)
    step_raw = projected[:, 2 * local_width + state_width :]
    rim_rows = passed_along(streams[row_count - CONV + 1 :], "ctx", 1)
    conv_taps = jnp.concatenate([input_conv, state_conv], axis=1)
    extended = jnp.concatenate([rim_rows, streams], axis=0)
    running = conv_taps[CONV] + conv_taps[0] * extended[0:row_count].astype(jnp.float32)
    for offset in range(1, CONV):
        running = running + conv_taps[offset] * extended[offset : offset + row_count].astype(
            jnp.float32
        )
    convolved = jax.nn.silu(running).astype(jnp.bfloat16)
    conv_inputs = convolved[:, :local_width]
    conv_states = convolved[:, local_width:]
    pieces = conv_states
    for bit_pos in range(level_count):
        partner = from_partner(pieces, "tp", bit_pos)
        lower = my_index // (1 << bit_pos) % 2 == 0
        pieces = jnp.where(
            lower,
            jnp.concatenate([pieces, partner], axis=1),
            jnp.concatenate([partner, pieces], axis=1),
        )
    blocks = row_count // SPAN
    write_vec = pieces[:, :NSTATE].astype(jnp.float32).reshape(blocks, SPAN, NSTATE)
    read_vec = pieces[:, NSTATE:].astype(jnp.float32).reshape(blocks, SPAN, NSTATE)
    step_size = jax.nn.softplus(step_raw + step_bias)
    log_damp = -step_size * jnp.exp(log_rate)
    inputs = conv_inputs.astype(jnp.float32).reshape(blocks, SPAN, heads_here, head_dim)
    cumulative, within, states = span_terms(
        inputs,
        step_size.reshape(blocks, SPAN, heads_here),
        log_damp.reshape(blocks, SPAN, heads_here),
        write_vec,
        read_vec,
    )
    zero_state = jnp.zeros((heads_here, head_dim, NSTATE), jnp.float32)
    block_state, across = span_pass(cumulative, states, read_vec, zero_state)
    span_logs = cumulative[:, -1, :]
    block_damp = jnp.exp(jnp.sum(span_logs, axis=0))

    def combine(earlier, later):
        return (earlier[0] * later[0], later[0][:, None, None] * earlier[1] + later[1])

    prefix = prefix_2(
        (block_damp, block_state),
        "ctx",
        combine,
        (jnp.ones_like(block_damp), jnp.zeros_like(block_state)),
    )
    incoming = prefix[1]
    offsets = jnp.cumsum(span_logs, axis=0) - span_logs
    carried_out = jnp.einsum(
        "kih,kin,hpn->kihp",
        jnp.exp(offsets[:, None, :] + cumulative),
        read_vec,
        incoming,
        precision=lax.Precision.HIGHEST,
    )
    outputs = within + across + carried_out + skip_gain[:, None] * inputs
    gate_out = outputs.reshape(row_count, local_width) * jax.nn.silu(gate_rows.astype(jnp.float32))
    square_sum = jnp.sum(gate_out * gate_out, axis=1)
    for bit_pos in range(level_count):
        square_sum = square_sum + from_partner(square_sum, "tp", bit_pos)
    mean_square = square_sum / (DINNER // GROUPS)
    normed = (gate_out * lax.rsqrt(mean_square + 1e-05)[:, None] * norm_gain).astype(jnp.bfloat16)
    mixed_out = lax.psum_scatter(
        jnp.dot(normed, out_weight, preferred_element_type=jnp.float32),
        "tp",
        scatter_dimension=0,
        tiled=True,
    )
    return mixed_out.astype(jnp.bfloat16)


def solution(mesh):
    placed = (
        P(("ctx", "tp"), None),
        P(None, "tp"),
        P(None, "tp"),
        P(None, "tp"),
        P(None, "tp"),
        P(None, "tp"),
        P(None, "tp"),
        P("tp"),
        P("tp"),
        P("tp"),
        P("tp"),
        P("tp", None),
    )
    return jax.shard_map(
        body, mesh=mesh, in_specs=placed, out_specs=P(("ctx", "tp"), None), check_vma=False
    )
```

profile of v0, /device:TPU:0, one launch (start us, length us, event | category | flops | bytes accessed | tf_op | source)
XLA Modules:
  0.0 332.7 jit_solution(3591740868698188273)
XLA Ops:
  7.4 1.4 copy.46
  11.0 51.9 %all-gather.5.cloned.1.call-done = bf16[512,4096]{1,0:T(8,128)(2,1)} async-done(((bf16[32,4096]{1,0:T(8,128)(2,1)}), bf16[512,4096]{1,0:T(8,128)(2,1)}) %all-gather.5.cloned.1.call-update) | async-done | bytes 4194320 | tf_op jit(solution)/shard_map/all_gather | solution.py:92
  62.8 25.3 %fusion.46 = (bf16[512,2192]{0,1:T(8,128)(2,1)}, f32[512,2192]{0,1:T(8,128)}) fusion(bf16[512,4096]{1,0:T(8,128)(2,1)} %all-gather.5.cloned.1.call-done, bf16[4096,16]{1,0:T(8,128)(2,1)S(1)} %copy.46, bf16[4096,128]{1,0:T(8,128)(2,1)} %param.19, bf16[4096,1024]{1,0:T(8,128)(2,1)} %param.18, bf16[4096,1024]{1,0:T(8,128)(2,1)} %param.17), kind=kOutput, calls=%fused_computation.82 | convolution fusion | flops 9266864128 | bytes 28884992 | tf_op jit(solution)/shard_map/dot_general | solution.py:91
  88.1 1.1 slice.75
  89.2 3.4 %collective-permute-start = (bf16[3,1152]{0,1:T(8,128)(2,1)S(1)}, bf16[3,1152]{0,1:T(8,128)(2,1)S(1)}, u32[]{:S(2)}, u32[]{:S(2)}) collective-permute-start(bf16[3,1152]{0,1:T(8,128)(2,1)S(1)} %slice.75), channel_id=1, source_target_pairs={{0,16},{1,17},{2,18},{3,19},{4,20},{5,21},{6,22},{7,23},{8,24},{9,... | collective-permute-start | bytes 20744 | tf_op jit(solution)/shard_map/ppermute | solution.py:16
  93.8 6.3 %fusion.47 = f32[8,64,16]{2,0,1:T(8,128)S(1)} fusion(f32[8,64,16]{2,0,1:T(8,128)S(1)} %copy.49), kind=kOutput, calls=%fused_computation.83 | output fusion | flops 516096 | bytes 65536 | tf_op jit(solution)/shard_map/jit(cumsum)/reduce_window_sum | solution.py:38
  100.1 2.4 slice.76
  102.7 6.0 %multiply_convert_fusion = bf16[512,1152]{0,1:T(8,128)(2,1)S(1)} fusion(bf16[512,1152]{0,1:T(8,128)(2,1)} %slice.76, bf16[3,1152]{0,1:T(8,128)(2,1)S(1)} %collective-permute-done, f32[1152]{0:T(1024)S(1)} %get-tuple-element.99, f32[1152]{0:T(1024)S(1)} %get-tuple-element.100, f32[1152]{0:T(1024)S(1)} %get-tuple-element.101, f32[1152]{0:T(1024)S(1)} %get-tuple-element.102, ...), kind=kLoop, calls=%fused_computation.29 | loop fusion | flops 15335424 | bytes 2389248 | tf_op jit(solution)/shard_map/convert_element_type | solution.py:108
  108.9 1.3 collective-permute-done.1
  113.6 2.8 reshape.54
  116.4 3.2 collective-permute-done.2
  119.6 1.3 maximum_select_fusion
  121.8 1.8 copy.48
  123.6 6.5 %fusion.12 = f32[8,16,64,256]{3,2,1,0:T(8,128)} fusion(bf16[8,64,256,1]{2,1,3,0:T(8,128)(2,1)} %bitcast.71, f32[8,64,16]{1,2,0:T(8,128)S(1)} %copy.56, bf16[8,64,16,64]{1,0,3,2:T(8,128)(2,1)S(1)} %reshape.54), kind=kOutput, calls=%fused_computation.17 | convolution fusion | flops 1611661312 | bytes 9732096 | tf_op jit(solution)/shard_map/kjh,kjhp,kjn->khpn/dot_general | solution.py:47
  130.1 20.3 %while.26 = (s32[]{:T(128)}, f32[16,64,256]{2,1,0:T(8,128)S(1)}, f32[8,16,64,256]{3,2,1,0:T(8,128)}, f32[8,16]{1,0:T(8,128)S(1)}, f32[8,16,64,256]{3,2,1,0:T(8,128)}, /*index=5*/s32[]{:T(128)}, s32[]{:T(128)}) while((s32[]{:T(128)}, f32[16,64,256]{2,1,0:T(8,128)S(1)}, f32[8,16,64,256]{3,2,1,0:T(8,128)}, f32[8,16]{1,0:T(8,128)S(1)}, ...), condition=%wide.region_2.3_spmd.clone, body=%wide.region_1.2_spmd.clone.sunk | while | flops 1048579 | bytes 5243680 | solution.py:57
  130.1 1.1 bitcast_dynamic-update-slice_fusion.2
  131.2 1.4 bitcast_add_fusion.6
  132.6 1.1 bitcast_dynamic-update-slice_fusion.2
  133.8 1.4 bitcast_add_fusion.6
  135.2 1.1 bitcast_dynamic-update-slice_fusion.2
  136.3 1.4 bitcast_add_fusion.6
  137.7 1.1 bitcast_dynamic-update-slice_fusion.2
  138.8 1.4 bitcast_add_fusion.6
  140.3 1.1 bitcast_dynamic-update-slice_fusion.2
  141.3 1.4 bitcast_add_fusion.6
  142.8 1.1 bitcast_dynamic-update-slice_fusion.2
  143.9 1.4 bitcast_add_fusion.6
  145.3 1.1 bitcast_dynamic-update-slice_fusion.2
  146.5 1.4 bitcast_add_fusion.6
  147.9 1.1 bitcast_dynamic-update-slice_fusion.2
  149.0 1.4 bitcast_add_fusion.6
  153.1 5.1 %all-reduce = f32[32]{0:T(128)S(1)} all-reduce(f32[32]{0:T(128)S(1)} %exponential_dynamic-update-slice_fusion), channel_id=2, replica_groups=mesh['ctx'=2,'tp'=16] {'ctx'}, use_global_device_ids=true, to_apply=%add | all-reduce | flops 32 | bytes 256
  158.3 1.1 copy.54
  160.5 1.1 copy.47
  161.6 1.2 fusion.48
  162.7 6.0 %fusion.15 = f32[8,16,64,64]{3,2,1,0:T(8,128)} fusion(f32[8,64,16]{1,2,0:T(8,128)S(1)} %copy.52, f32[8,64,16]{1,2,0:T(8,128)S(1)} %copy.50, f32[8,64,64]{2,1,0:T(8,128)S(1)} %fusion.48, pred[64,64]{1,0:T(8,128)(4,1)S(1)} %iota_compare_fusion, bf16[8,64,16,64]{1,0,3,2:T(8,128)(2,1)S(1)} %reshape.54), kind=kOutput, calls=%fused_computation.21 | convolution fusion | flops 404750336 | bytes 3346432 | tf_op jit(solution)/shard_map/kijh,kjhp->kihp/dot_general | solution.py:45
  168.7 13.6 %all-gather.7.cloned.1.call-done = f32[32,64,256]{2,1,0:T(8,128)} async-done(((f32[16,64,256]{2,1,0:T(8,128)}), f32[32,64,256]{2,1,0:T(8,128)}) %all-gather.7.cloned.1.call-update) | async-done | bytes 2097168 | tf_op jit(solution)/shard_map/all_gather | solution.py:25
  182.4 1.9 fusion.37
  184.6 7.3 %fusion.13 = f32[8,64,16,64]{1,3,2,0:T(8,128)S(1)} fusion(f32[8,16,64,64]{3,2,1,0:T(8,128)S(1)} %copy-done.1, f32[8,64,16,64]{1,3,2,0:T(8,128)S(1)} %fusion.37, bf16[8,64,256,1]{2,1,3,0:T(8,128)(2,1)S(1)} %bitcast.70, f32[8,16,64,256]{3,2,1,0:T(8,128)} %get-tuple-element.77, f32[16]{0:T(128)S(1)} %copy-done.3, f32[8,64,16]{1,2,0:T(8,128)S(1)} %copy.59, ...), kind=kOutput, calls=%fused_computation.18 | convolution fusion | flops 1614282752 | bytes 16056384 | tf_op jit(solution)/shard_map/kih,kin,khpn->kihp/dot_general | solution.py:58
  191.9 5.2 %copy.61 = f32[8,64,16,64]{1,0,3,2:T(8,128)} copy(f32[8,64,16,64]{1,3,2,0:T(8,128)S(1)} %fusion.13) | data formatting | bytes 4194304 | tf_op jit(solution)/shard_map/add | solution.py:156
  197.1 3.4 %reshape.58 = f32[512,1024]{0,1:T(8,128)S(1)} reshape(f32[8,64,16,64]{1,0,3,2:T(8,128)} %copy.61) | data formatting | bytes 4194304 | tf_op jit(solution)/shard_map/reshape | solution.py:157
  200.6 2.1 multiply_reduce_fusion
  202.7 1.1 collective-permute-done.3
  203.9 1.5 collective-permute-start.4
  205.4 2.1 collective-permute-done.4
  207.5 10.5 %fusion.36 = f32[512,4096]{1,0:T(8,128)} fusion(bf16[1024,4096]{1,0:T(8,128)(2,1)} %param.27, f32[1024]{0:T(1024)S(1)} %copy-done.5, f32[512]{0:T(512)S(1)} %add_rsqrt_fusion, f32[512,1024]{0,1:T(8,128)S(1)} %reshape.58, bf16[512,2192]{0,1:T(8,128)(2,1)S(1)} %copy-done.2), kind=kOutput, calls=%fused_computation.52 | convolution fusion | flops 4299685888 | bytes 19929088 | tf_op jit(solution)/shard_map/dot_general | solution.py:164
  218.0 106.4 %reduce-scatter.2.cloned.1.call-done = f32[32,4096]{1,0:T(8,128)} async-done(((f32[512,4096]{1,0:T(8,128)}), f32[32,4096]{1,0:T(8,128)}) %reduce-scatter.2.cloned.1.call-update) | async-done | bytes 524304 | tf_op jit(solution)/shard_map/reduce_scatter | solution.py:163
  324.4 1.8 convert_element_type.36
  (65 shorter events, 12.2 us)
Async XLA Ops:
  6.5 56.3 %all-gather.5.cloned.1.call-start = ((), (), s32[]{:S(2)}) async-start(), calls=%async_computation.1 | async-start | bytes 4456448 | tf_op jit(solution)/shard_map/all_gather | solution.py:92
  7.3 175.0 %all-gather.7.cloned.1.call-start = ((), (), s32[]{:S(2)}) async-start(), calls=%async_computation.3 | async-start | bytes 3145728 | tf_op jit(solution)/shard_map/all_gather | solution.py:25
  10.9 81.7 %copy-start.4 = (f32[16]{0:T(128)S(1)}, f32[16]{0:T(128)}, u32[]{:S(2)}) copy-start(f32[16]{0:T(128)} %param.24) | copy-start | bytes 196
  89.2 13.5 %collective-permute-start = (bf16[3,1152]{0,1:T(8,128)(2,1)S(1)}, bf16[3,1152]{0,1:T(8,128)(2,1)S(1)}, u32[]{:S(2)}, u32[]{:S(2)}) collective-permute-start(bf16[3,1152]{0,1:T(8,128)(2,1)S(1)} %slice.75), channel_id=1, source_target_pairs={{0,16},{1,17},{2,18},{3,19},{4,20},{5,21},{6,22},{7,23},{8,24},{9,... | collective-permute-start | bytes 20744 | tf_op jit(solution)/shard_map/ppermute | solution.py:16
  108.8 1.4 collective-permute-start.1
  111.0 8.7 %collective-permute-start.2 = (bf16[512,256]{0,1:T(8,128)(2,1)}, bf16[512,256]{0,1:T(8,128)(2,1)}, u32[]{:S(2)}, u32[]{:S(2)}) collective-permute-start(bf16[512,256]{0,1:T(8,128)(2,1)} %maximum_select_fusion.1), channel_id=1, source_target_pairs={{0,2},{1,3},{2,0},{3,1},{4,6},{5,7},{6,4},{7,5},{8,10},{9,11},{10,... | collective-permute-start | bytes 786440 | tf_op jit(solution)/shard_map/ppermute | solution.py:20
  130.1 21.4 %copy-start.6 = (u32[32]{0:T(128)S(1)}, u32[32]{0:T(128)}, u32[]{:S(2)}) copy-start(u32[32]{0:T(128)} %constant.100) | copy-start | bytes 388
  150.4 1.0 copy-start
  151.4 173.0 %reduce-scatter.2.cloned.1.call-start = ((), (), s32[]{:S(2)}) async-start(), calls=%async_computation.2 | async-start | bytes 8912896 | tf_op jit(solution)/shard_map/reduce_scatter | solution.py:163
  182.4 2.2 copy-start.1
  182.4 2.2 copy-start.3
  200.6 6.9 %copy-start.2 = (bf16[512,2192]{0,1:T(8,128)(2,1)S(1)}, bf16[512,2192]{0,1:T(8,128)(2,1)}, u32[]{:S(2)}) copy-start(bf16[512,2192]{0,1:T(8,128)(2,1)} %get-tuple-element.133) | copy-start | bytes 6733828
  200.6 6.9 %copy-start.5 = (f32[1024]{0:T(1024)S(1)}, f32[1024]{0:T(1024)}, u32[]{:S(2)}) copy-start(f32[1024]{0:T(1024)} %param.26) | copy-start | bytes 12292
  202.7 1.2 collective-permute-start.3
  203.9 3.6 %collective-permute-start.4 = (f32[512]{0:T(512)S(1)}, f32[512]{0:T(512)S(1)}, u32[]{:S(2)}, u32[]{:S(2)}) collective-permute-start(f32[512]{0:T(512)S(1)} %add.121), channel_id=1, source_target_pairs={{0,2},{1,3},{2,0},{3,1},{4,6},{5,7},{6,4},{7,5},{8,10},{9,11},{10,... | collective-permute-start | bytes 6152 | tf_op jit(solution)/shard_map/ppermute | solution.py:20
Sparse Core Ops, SparseCore 0:
  9.5 53.2 all-gather.4
  151.5 30.6 all-gather.6
  218.2 106.1 reduce-scatter.1
where the time goes:
time: 334 us; the launch traced here: 333 us
  waiting for transfers between devices  180 us (54%)
  matrix products  58.7 us (18%)
  other arithmetic  40.3 us (12%)
  local copies, waits for them, and re-layouts  28.3 us (8%)
  between operations  14.2 us (4%)
  starting transfers between devices  5.64 us (2%)
  blocking collectives  5.1 us (2%)
    reduce_scatter x1, waiting for transfers between devices, body(): lax.psum_scatter(jnp.dot(normed, out_weight, preferred_element_type=jnp.f...  106 us
    all_gather x1, waiting for transfers between devices, body(): lax.all_gather(tokens, 'tp', axis=0, tiled=True)  51.9 us
    dot_general x1, matrix products, body(): jnp.dot(lax.all_gather(tokens, 'tp', axis=0, tiled=True), combined, prefe...  25.3 us
    all_gather x1, waiting for transfers between devices, prefix_2(): gathered = jax.tree.map(lambda a: lax.all_gather(a, axis), part)  13.6 us
    add x8, other arithmetic, advance(): return (factor[:, None, None] * carried + increment, carried)  11.3 us
    dot_general x1, matrix products, body(): jnp.dot(normed, out_weight, preferred_element_type=jnp.float32)  10.5 us
    dynamic_update_slice x8, other arithmetic, span_pass(): lax.scan(advance, zero_state, (jnp.exp(cumulative[:, -1, :]), states))  8.81 us
    ppermute x4, waiting for transfers between devices, from_partner(): lax.ppermute(array, axis, [(i, i ^ 1 << distance) for i in range(lax.axis...  7.79 us
  transfers between devices with their start and end apart: 8, of which 7 were waited for; matrix products, arithmetic and copies ran while one was open for 9% of the time, Pallas kernels for 0%

commit v1 on v0

v1 whole, which is shorter than its diff:
```python
import functools

import jax
import jax.numpy as jnp
from jax import lax
from jax.experimental import pallas as pl
from jax.experimental.pallas import tpu as pltpu
from jax.sharding import PartitionSpec as P

NSTATE = 256
GROUPS = 4
CONV = 4
DINNER = 16384
CHUNK = 128
MESH = pl.DeviceIdType.MESH
HIGH = lax.Precision.HIGHEST
F32 = jnp.float32
BF16 = jnp.bfloat16
VMEM = pl.BlockSpec(memory_space=pltpu.VMEM)
ANY = pl.BlockSpec(memory_space=pl.ANY)


def passed_along(array, axis, by):
    peers = lax.axis_size(axis)
    pairs = [(i, i + by) for i in range(peers) if 0 <= i + by < peers]
    return lax.ppermute(array, axis, pairs)


def from_partner(array, axis, distance):
    return lax.ppermute(array, axis, [(i, i ^ 1 << distance) for i in range(lax.axis_size(axis))])


def two_parts(value):
    high = value.astype(BF16)
    return high, (value - high.astype(F32)).astype(BF16)


def ssd_kernel(x_ref, bc_ref, dt_ref, la_ref, dtt_ref, lat_ref, e_ref, y_ref, st_ref, cum_ref):
    rows, width = x_ref.shape
    heads = dt_ref.shape[1]
    head_dim = width // heads
    q = CHUNK
    st_ref[...] = jnp.zeros_like(st_ref)
    row = lax.broadcasted_iota(jnp.int32, (q, q), 0)
    col = lax.broadcasted_iota(jnp.int32, (q, q), 1)
    causal = row >= col
    lower = causal.astype(F32)
    upper = (row <= col).astype(F32)
    first = lax.broadcasted_iota(jnp.int32, (q, 2 * head_dim), 1) < head_dim
    spread_out = e_ref[...]
    offset = jnp.zeros((1, heads), F32)
    for k in range(rows // q):
        at = pl.ds(k * q, q)
        cum = jnp.dot(lower, la_ref[at, :], precision=HIGH, preferred_element_type=F32)
        cumt = jnp.dot(lat_ref[:, at], upper, precision=HIGH, preferred_element_type=F32)
        cum_ref[at, :] = cum + offset
        last = cum[q - 1 : q, :]
        offset = offset + last
        dtt = dtt_ref[:, at]
        write = bc_ref[at, :NSTATE]
        read = bc_ref[at, NSTATE:]
        scores = lax.dot_general(read, write, (((1,), (1,)), ((), ())), preferred_element_type=F32)
        scores = jnp.where(causal, scores, 0.0)
        grow = jnp.dot(jnp.exp(cum), spread_out, precision=HIGH, preferred_element_type=F32)
        weight = jnp.dot(
            jnp.exp(last - cum) * dt_ref[at, :], spread_out, precision=HIGH, preferred_element_type=F32
        )
        x = x_ref[at, :]
        if k > 0:
            high, low = two_parts(st_ref[...])
            across = jnp.dot(read, high, preferred_element_type=F32)
            y_ref[at, :] = grow * (across + jnp.dot(read, low, preferred_element_type=F32))
        for h in range(0, heads, 2):
            mixes = []
            for i in (h, h + 1):
                gap = jnp.minimum(cum[:, i : i + 1] - cumt[i : i + 1, :], 0.0)
                mixes.append(scores * jnp.exp(gap) * dtt[i : i + 1, :])
            lanes = slice(h * head_dim, (h + 2) * head_dim)
            pair = x[:, lanes]
            none = jnp.zeros_like(pair)
            stacked = jnp.concatenate([jnp.where(first, pair, none), jnp.where(first, none, pair)], axis=0)
            high, low = two_parts(jnp.concatenate(mixes, axis=1))
            within = jnp.dot(high, stacked, preferred_element_type=F32)
            within = within + jnp.dot(low, stacked, preferred_element_type=F32)
            if k > 0:
                y_ref[at, lanes] += within
            else:
                y_ref[at, lanes] = within
        high, low = two_parts(x.astype(F32) * weight)
        over_rows = (((0,), (0,)), ((), ()))
        added = lax.dot_general(write, high, over_rows, preferred_element_type=F32)
        added = added + lax.dot_general(write, low, over_rows, preferred_element_type=F32)
        st_ref[...] = grow[q - 1 : q, :] * st_ref[...] + added


def gate_kernel(y_ref, cum_ref, bc_ref, inc_ref, x_ref, skip_ref, gate_ref, e_ref, go_ref, sq_ref):
    grow = jnp.dot(jnp.exp(cum_ref[...]), e_ref[...], precision=HIGH, preferred_element_type=F32)
    carried = jnp.dot(bc_ref[:, NSTATE:], inc_ref[...], preferred_element_type=F32)
    y = y_ref[...] + grow * carried + skip_ref[...] * x_ref[...].astype(F32)
    out = y * jax.nn.silu(gate_ref[...].astype(F32))
    go_ref[...] = out
    sq_ref[...] = jnp.sum(out * out, axis=1, keepdims=True)


def out_kernel(
    size_a, size_b, steps, go_ref, r_ref, gain_ref, w_hbm, o_ref,
    normed, w_ref, own, send1, recv1, send2, recv2, send3, recv3,
    w_sem, s1, r1, s2, r2, s3, r3,
):
    me = lax.axis_index("tp")
    a = me // (2 * size_b)
    b = me // 2 % size_b
    c = me % 2
    sibling = me + 1 - 2 * c
    blocks = size_a * size_b
    rows = normed.shape[0]
    part = rows // (2 * blocks)
    wide = w_ref.shape[2]

    def peer_b(i):
        return a * (2 * size_b) + (b + i) % size_b * 2 + c

    def peer_a(i):
        return (a + i) % size_a * (2 * size_b) + b * 2 + c

    def w_copy(k):
        return pltpu.make_async_copy(
            w_hbm.at[:, pl.ds(pl.multiple_of(k * wide, wide), wide)], w_ref.at[k], w_sem.at[k]
        )

    for k in range(steps):
        w_copy(k).start()
    barrier = pltpu.get_barrier_semaphore()
    pl.semaphore_signal(barrier, inc=1, device_id={"tp": sibling}, device_id_type=MESH)
    for i in range(1, size_b):
        pl.semaphore_signal(barrier, inc=1, device_id={"tp": peer_b(i)}, device_id_type=MESH)
    for i in range(1, size_a):
        pl.semaphore_signal(barrier, inc=1, device_id={"tp": peer_a(i)}, device_id_type=MESH)

    normed[...] = (go_ref[...] * r_ref[...] * gain_ref[...]).astype(BF16)
    pl.semaphore_wait(barrier, size_a + size_b - 1)

    def copy1(k):
        return pltpu.make_async_remote_copy(
            src_ref=send1.at[k], dst_ref=recv1.at[k], send_sem=s1.at[k], recv_sem=r1.at[k],
            device_id={"tp": sibling}, device_id_type=MESH,
        )

    def copy2(k, i):
        return pltpu.make_async_remote_copy(
            src_ref=send2.at[i - 1, k], dst_ref=recv2.at[i - 1, k],
            send_sem=s2.at[i - 1, k], recv_sem=r2.at[i - 1, k],
            device_id={"tp": peer_b(i)}, device_id_type=MESH,
        )

    def copy3(k, i):
        return pltpu.make_async_remote_copy(
            src_ref=send3.at[i - 1, k], dst_ref=recv3.at[i - 1, k],
            send_sem=s3.at[i - 1, k], recv_sem=r3.at[i - 1, k],
            device_id={"tp": peer_a(i)}, device_id_type=MESH,
        )

    def rows_of(core):
        return jnp.concatenate(
            [normed[pl.ds(pl.multiple_of((j * 2 + core) * part, part), part), :] for j in range(blocks)], axis=0
        )

    def step(k, carry):
        @pl.when(k < steps)
        def _():
            w_copy(k).wait()
            theirs = jnp.dot(rows_of(1 - c), w_ref[k], preferred_element_type=F32)
            send1[k] = theirs
            copy1(k).start()
            mine = jnp.dot(rows_of(c), w_ref[k], preferred_element_type=F32)
            own[k] = mine.reshape(size_a, size_b, part, wide)

        @pl.when((k >= 1) & (k < steps + 1))
        def _():
            j = k - 1
            copy1(j).wait_recv()
            own[j] += recv1[j].astype(F32).reshape(size_a, size_b, part, wide)
            for i in range(1, size_b):
                send2[i - 1, j] = own[j, :, (b + i) % size_b]
                copy2(j, i).start()

        @pl.when((k >= 2) & (k < steps + 2))
        def _():
            j = k - 2
            mine = own[j, :, b]
            for i in range(1, size_b):
                copy2(j, i).wait_recv()
                mine = mine + recv2[i - 1, j].astype(F32)
            own[j, :, b] = mine
            for i in range(1, size_a):
                send3[i - 1, j] = own[j, (a + i) % size_a, b].astype(BF16)
                copy3(j, i).start()

        @pl.when(k >= 3)
        def _():
            j = k - 3
            mine = own[j, a, b]
            for i in range(1, size_a):
                copy3(j, i).wait_recv()
                mine = mine + recv3[i - 1, j].astype(F32)
            o_ref[:, pl.ds(pl.multiple_of(j * wide, wide), wide)] = mine.astype(BF16)

        return carry

    lax.fori_loop(0, steps + 3, step, 0)

    def drain(k, carry):
        copy1(k).wait_send()
        for i in range(1, size_b):
            copy2(k, i).wait_send()
        for i in range(1, size_a):
            copy3(k, i).wait_send()
        return carry

    lax.fori_loop(0, steps, drain, 0)


def project_out(go, r, gain, weight, tp):
    rows = go.shape[0]
    depth, columns = weight.shape
    size_a = 4
    size_b = tp // (2 * size_a)
    steps = 8
    wide = columns // steps
    part = rows // tp
    half = rows // 2
    dma = pltpu.SemaphoreType.DMA
    return pl.pallas_call(
        functools.partial(out_kernel, size_a, size_b, steps),
        out_shape=jax.ShapeDtypeStruct((part, columns), BF16),
        in_specs=[VMEM, VMEM, VMEM, ANY],
        out_specs=VMEM,
        scratch_shapes=[
            pltpu.VMEM((rows, depth), BF16),
            pltpu.VMEM((steps, depth, wide), BF16),
            pltpu.VMEM((steps, size_a, size_b, part, wide), F32),
            pltpu.VMEM((steps, half, wide), F32),
            pltpu.VMEM((steps, half, wide), F32),
            pltpu.VMEM((size_b - 1, steps, size_a, part, wide), F32),
            pltpu.VMEM((size_b - 1, steps, size_a, part, wide), F32),
            pltpu.VMEM((size_a - 1, steps, part, wide), BF16),
            pltpu.VMEM((size_a - 1, steps, part, wide), BF16),
            dma((steps,)), dma((steps,)), dma((steps,)),
            dma((size_b - 1, steps)), dma((size_b - 1, steps)),
            dma((size_a - 1, steps)), dma((size_a - 1, steps)),
        ],
        compiler_params=pltpu.CompilerParams(
            collective_id=1, has_side_effects=True, vmem_limit_bytes=50 * 1024 * 1024
        ),
    )(go, r, gain, weight)


def body(
    tokens, gate_weight, input_weight, state_weight, step_weight, input_conv, state_conv,
    log_rate, step_bias, skip_gain, norm_gain, out_weight,
):
    tensor_size = lax.axis_size("tp")
    ctx_size = lax.axis_size("ctx")
    per_group = tensor_size // GROUPS
    level_count = per_group.bit_length() - 1
    my_index = lax.axis_index("tp")
    local_width = gate_weight.shape[1]
    state_width = state_weight.shape[1]
    heads = log_rate.shape[0]
    head_dim = local_width // heads
    combined = jnp.concatenate([gate_weight, input_weight, state_weight, step_weight], axis=1)
    projected = jnp.dot(
        lax.all_gather(tokens, "tp", axis=0, tiled=True), combined, preferred_element_type=F32
    )
    rows = projected.shape[0]
    gate_rows = projected[:, :local_width].astype(BF16)
    streams = projected[:, local_width : 2 * local_width + state_width].astype(BF16)
    step_raw = projected[:, 2 * local_width + state_width :]
    rim_rows = passed_along(streams[rows - CONV + 1 :], "ctx", 1)
    conv_taps = jnp.concatenate([input_conv, state_conv], axis=1)
    extended = jnp.concatenate([rim_rows, streams], axis=0)
    running = conv_taps[CONV] + conv_taps[0] * extended[0:rows].astype(F32)
    for offset in range(1, CONV):
        running = running + conv_taps[offset] * extended[offset : offset + rows].astype(F32)
    convolved = jax.nn.silu(running).astype(BF16)
    conv_inputs = convolved[:, :local_width]
    pieces = convolved[:, local_width:]
    for bit_pos in range(level_count):
        partner = from_partner(pieces, "tp", bit_pos)
        lower = my_index // (1 << bit_pos) % 2 == 0
        pieces = jnp.where(
            lower,
            jnp.concatenate([pieces, partner], axis=1),
            jnp.concatenate([partner, pieces], axis=1),
        )
    step_size = jax.nn.softplus(step_raw + step_bias)
    log_damp = -step_size * jnp.exp(log_rate)
    spread_out = jnp.repeat(jnp.eye(heads, dtype=F32), head_dim, axis=1)

    local_y, block_state, cumulative = pl.pallas_call(
        ssd_kernel,
        out_shape=(
            jax.ShapeDtypeStruct((rows, local_width), F32),
            jax.ShapeDtypeStruct((NSTATE, local_width), F32),
            jax.ShapeDtypeStruct((rows, heads), F32),
        ),
        in_specs=[VMEM] * 7,
        out_specs=(VMEM, VMEM, VMEM),
        compiler_params=pltpu.CompilerParams(vmem_limit_bytes=40 * 1024 * 1024),
    )(conv_inputs, pieces, step_size, log_damp, step_size.T, log_damp.T, spread_out)

    sent_state = block_state.astype(BF16)
    if ctx_size == 2:
        incoming = passed_along(sent_state, "ctx", 1)
    else:
        damps = lax.all_gather(jnp.repeat(jnp.exp(cumulative[-1]), head_dim), "ctx")
        states = lax.all_gather(sent_state, "ctx")

        def one(hop, state):
            return damps[hop][None, :] * state + states[hop].astype(F32)

        incoming = lax.fori_loop(
            0, lax.axis_index("ctx"), one, jnp.zeros((NSTATE, local_width), F32)
        ).astype(BF16)

    def by_rows(width):
        return pl.BlockSpec((CHUNK, width), lambda i: (i, 0))

    def whole(array):
        return pl.BlockSpec(array.shape, lambda i: (0, 0))

    skip = jnp.repeat(skip_gain, head_dim)[None, :]
    gate_out, square_sum = pl.pallas_call(
        gate_kernel,
        grid=(rows // CHUNK,),
        out_shape=(
            jax.ShapeDtypeStruct((rows, local_width), F32),
            jax.ShapeDtypeStruct((rows, 1), F32),
        ),
        in_specs=[
            by_rows(local_width), by_rows(heads), by_rows(2 * NSTATE), whole(incoming),
            by_rows(local_width), whole(skip), by_rows(local_width), whole(spread_out),
        ],
        out_specs=(by_rows(local_width), by_rows(1)),
        compiler_params=pltpu.CompilerParams(vmem_limit_bytes=40 * 1024 * 1024),
    )(local_y, cumulative, pieces, incoming, conv_inputs, skip, gate_rows, spread_out)
    square_sum = square_sum[:, 0]
    for bit_pos in range(level_count):
        square_sum = square_sum + from_partner(square_sum, "tp", bit_pos)
    mean_square = square_sum / (DINNER // GROUPS)
    inverse = lax.rsqrt(mean_square + 1e-05)[:, None]
    return project_out(gate_out, inverse, norm_gain[None, :], out_weight, tensor_size)


def solution(mesh):
    placed = (
        P(("ctx", "tp"), None),
        P(None, "tp"),
        P(None, "tp"),
        P(None, "tp"),
        P(None, "tp"),
        P(None, "tp"),
        P(None, "tp"),
        P("tp"),
        P("tp"),
        P("tp"),
        P("tp"),
        P("tp", None),
    )
    return jax.shard_map(
        body, mesh=mesh, in_specs=placed, out_specs=P(("ctx", "tp"), None), check_vma=False
    )
```

time: 334 us -> 202 us (0.60)
  waiting for transfers between devices: 180 us -> 73.8 us
  Pallas kernels: 0 us -> 66.5 us
  other arithmetic: 40.3 us -> 3.29 us
  matrix products: 58.7 us -> 22.6 us
  local copies, waits for them, and re-layouts: 28.3 us -> 12.5 us
  blocking collectives: 5.1 us -> 0 us
  starting transfers between devices: 5.64 us -> 9.12 us
    reduce_scatter x1 -> x0, waiting for transfers between devices: 106 us -> none  [body(): lax.psum_scatter(jnp.dot(normed, out_weight, preferred_element_type=jnp.f...]
    pallas_call x0 -> x3, Pallas kernels: none -> 66.5 us  [the longest x1 56.2 us: project_out(): pl.pallas_call(functools.partial(out_kernel, size_a, size_b, steps), out_...]
    dot_general x6 -> x0, matrix products: 33.4 us -> none  [the longest x1 10.5 us: body(): jnp.dot(normed, out_weight, preferred_element_type=jnp.float32)]
    all_gather x1 -> x0, waiting for transfers between devices: 13.6 us -> none  [prefix_2(): gathered = jax.tree.map(lambda a: lax.all_gather(a, axis), part)]
    add x9 -> x0, other arithmetic: 11.3 us -> none  [the longest x8 11.3 us: advance(): return (factor[:, None, None] * carried + increment, carried)]
    ppermute x1 -> x2, waiting for transfers between devices: 0.01 us -> 9.98 us  [passed_along(): return lax.ppermute(array, axis, pairs)]
    dynamic_update_slice x8 -> x0, other arithmetic: 8.81 us -> none  [span_pass(): lax.scan(advance, zero_state, (jnp.exp(cumulative[:, -1, :]), states))]
    another operation x2 -> x0, other arithmetic: 6.35 us -> none  [the longest x1 6.33 us: span_terms(): cumulative = jnp.cumsum(log_damp, axis=1)]
  transfers between devices with their start and end apart: 8 -> 7, of which waited for: 7 -> 7; matrix products, arithmetic and copies ran while one was open for 9% -> 4% of each run, Pallas kernels for 0% -> 0%
where the time goes in v1:
time: 202 us; the launch traced here: 201 us
  waiting for transfers between devices  73.8 us (37%)
  Pallas kernels  66.5 us (33%)
  matrix products  22.6 us (11%)
  between operations  13.6 us (7%)
  local copies, waits for them, and re-layouts  12.5 us (6%)
  starting transfers between devices  9.12 us (5%)
  other arithmetic  3.29 us (2%)
    pallas_call x1, Pallas kernels, project_out(): pl.pallas_call(functools.partial(out_kernel, size_a, size_b, steps), out_...  56.2 us
    all_gather x1, waiting for transfers between devices, body(): lax.all_gather(tokens, 'tp', axis=0, tiled=True)  52.7 us
    dot_general x1, matrix products, body(): jnp.dot(lax.all_gather(tokens, 'tp', axis=0, tiled=True), combined, prefe...  22.6 us
    ppermute x4, waiting for transfers between devices, from_partner(): lax.ppermute(array, axis, [(i, i ^ 1 << distance) for i in range(lax.axis...  10.4 us
    ppermute x2, waiting for transfers between devices, passed_along(): return lax.ppermute(array, axis, pairs)  9.98 us
    unnamed x23, local copies, waits for them, and re-layouts  8.18 us
    ppermute x2, starting transfers between devices, passed_along(): return lax.ppermute(array, axis, pairs)  7.78 us
    pallas_call x1, Pallas kernels, body(): pl.pallas_call(ssd_kernel, out_shape=(jax.ShapeDtypeStruct((rows, local_w...  7.12 us
  transfers between devices with their start and end apart: 7, of which 7 were waited for; matrix products, arithmetic and copies ran while one was open for 4% of the time, Pallas kernels for 0%

profile of v1, /device:TPU:0, one launch (start us, length us, event | category | flops | bytes accessed | tf_op | source)
XLA Modules:
  0.0 201.5 jit_solution(2218147575349392953)
XLA Ops:
  6.5 0.0 all-gather.2.cloned.1.call-start
  6.5 0.7 all-gather.2.cloned.1.call-update
  7.3 1.4 copy.22
  8.6 0.8 constant_dynamic-update-slice_fusion.1
  9.4 0.7 constant_dynamic-update-slice_fusion
  10.1 52.7 %all-gather.2.cloned.1.call-done = bf16[512,4096]{1,0:T(8,128)(2,1)} async-done(((bf16[32,4096]{1,0:T(8,128)(2,1)}), bf16[512,4096]{1,0:T(8,128)(2,1)}) %all-gather.2.cloned.1.call-update) | async-done | bytes 4194320 | tf_op jit(solution)/shard_map/all_gather | solution.py:273
  62.8 22.6 %fusion.15 = (bf16[512,2192]{1,0:T(8,128)(2,1)S(1)}, f32[512,2192]{1,0:T(8,128)}) fusion(bf16[512,4096]{1,0:T(8,128)(2,1)} %all-gather.2.cloned.1.call-done, bf16[4096,16]{1,0:T(8,128)(2,1)S(1)} %copy.22, bf16[4096,128]{1,0:T(8,128)(2,1)} %param.15, bf16[4096,1024]{1,0:T(8,128)(2,1)} %param.14, bf16[4096,1024]{1,0:T(8,128)(2,1)} %param.13), kind=kOutput, calls=%fused_computation.31 | convolution fusion | flops 9266864128 | bytes 28884992 | tf_op jit(solution)/shard_map/dot_general | solution.py:272
  85.4 3.6 %collective-permute-start = (bf16[3,1152]{1,0:T(4,128)(2,1)S(1)}, bf16[3,1152]{1,0:T(4,128)(2,1)S(1)}, u32[]{:S(2)}, u32[]{:S(2)}) collective-permute-start(bf16[3,1152]{1,0:T(4,128)(2,1)S(1)} %slice.61), channel_id=1, source_target_pairs={{0,16},{1,17},{2,18},{3,19},{4,20},{5,21},{6,22},{7,23},{8,24},{9,... | collective-permute-start | bytes 20744 | tf_op jit(solution)/shard_map/ppermute | solution.py:26
  89.0 0.1 slice_reduce_fusion.4
  89.1 0.0 copy-start.9
  89.1 0.1 slice.62
  89.2 0.0 copy-start.7
  89.2 1.0 collective-permute-done
  90.2 1.7 multiply_convert_fusion
  91.9 0.0 copy-done.6
  91.9 1.0 copy-done.5
  92.9 0.1 collective-permute-start.1
  93.0 1.3 collective-permute-done.1
  94.4 0.1 maximum_select_fusion.1
  94.5 0.6 collective-permute-start.2
  95.1 0.1 broadcast_in_dim.16
  95.2 0.1 reshape.7.e_ref
  95.3 1.1 negate_multiply_fusion
  96.4 0.1 copy.25.dtt_ref
  96.5 0.1 copy.26.lat_ref
  96.6 1.3 slice.70.x_ref
  97.9 0.0 copy-start.8
  98.0 4.9 %collective-permute-done.2 = bf16[512,256]{1,0:T(8,128)(2,1)S(1)} collective-permute-done((bf16[512,256]{1,0:T(8,128)(2,1)S(1)}, bf16[512,256]{1,0:T(8,128)(2,1)S(1)}, u32[]{:S(2)}, u32[]{:S(2)}) %collective-permute-start.2) | collective-permute-done | bytes 262176 | tf_op jit(solution)/shard_map/ppermute | solution.py:30
  102.9 0.1 maximum_select_fusion.bc_ref
  103.0 7.1 %shard_map.118 = (f32[512,1024]{1,0:T(8,128)S(1)}, f32[256,1024]{1,0:T(8,128)S(1)}, f32[512,16]{1,0:T(8,128)S(1)}) custom-call(bf16[512,1024]{1,0:T(8,128)(2,1)S(1)} %slice.70.x_ref, bf16[512,512]{1,0:T(8,128)(2,1)S(1)} %maximum_select_fusion.bc_ref, f32[512,16]{1,0:T(8,128)S(1)} %get-tuple-element.21.dt_ref, f32[512,16]{1,0:T(8,128)S(1)} %get-tuple-element.20.la_ref, ...), custom_call_target="tpu_custom_call" | custom-call | tf_op jit(solution)/shard_map/pallas_call | solution.py:300
  110.1 1.3 copy-done.2
  111.5 0.1 convert_element_type.31
  111.6 4.2 %collective-permute-start.3 = (bf16[256,1024]{1,0:T(8,128)(2,1)S(1)}, bf16[256,1024]{1,0:T(8,128)(2,1)S(1)}, u32[]{:S(2)}, u32[]{:S(2)}) collective-permute-start(bf16[256,1024]{1,0:T(8,128)(2,1)S(1)} %convert_element_type.31), channel_id=1, source_target_pairs={{0,16},{1,17},{2,18},{3,19},{4,20},{5,21},{6,22},{7,23},{8,24},{9,... | collective-permute-start | bytes 1572872 | tf_op jit(solution)/shard_map/ppermute | solution.py:26
  115.8 0.1 broadcast_in_dim.17
  115.9 0.1 broadcast_in_dim_reshape.3.skip_ref
  116.0 1.4 slice.73.gate_ref
  117.4 9.0 %collective-permute-done.3.inc_ref = bf16[256,1024]{1,0:T(8,128)(2,1)S(1)} collective-permute-done((bf16[256,1024]{1,0:T(8,128)(2,1)S(1)}, bf16[256,1024]{1,0:T(8,128)(2,1)S(1)}, u32[]{:S(2)}, u32[]{:S(2)}) %collective-permute-start.3) | collective-permute-done | bytes 524320 | tf_op jit(solution)/shard_map/ppermute | solution.py:26
  126.4 3.2 %shard_map.119 = (f32[512,1024]{1,0:T(8,128)S(1)}, f32[512,1]{1,0:T(8,128)S(1)}) custom-call(f32[512,1024]{1,0:T(8,128)S(1)} %copy-done.3, f32[512,16]{1,0:T(8,128)S(1)} %get-tuple-element.11.cum_ref, bf16[512,512]{1,0:T(8,128)(2,1)S(1)} %maximum_select_fusion.bc_ref, bf16[256,1024]{1,0:T(8,128)(2,1)S(1)} %collective-permute-done.3.inc_ref, ...), custom_call_target="tpu_custom_call" | custom-call | tf_op jit(solution)/shard_map/pallas_call | solution.py:333
  129.6 1.3 copy-done
  130.9 0.1 reduce.5
  131.1 0.1 collective-permute-start.4
  131.2 1.1 collective-permute-done.4
  132.3 0.6 collective-permute-start.5
  132.9 3.0 %collective-permute-done.5 = f32[512]{0:T(512)S(1)} collective-permute-done((f32[512]{0:T(512)S(1)}, f32[512]{0:T(512)S(1)}, u32[]{:S(2)}, u32[]{:S(2)}) %collective-permute-start.5) | collective-permute-done | bytes 2080 | tf_op jit(solution)/shard_map/ppermute | solution.py:30
  135.9 0.2 copy.27.r_ref
  136.1 1.6 copy-done.1
  137.7 56.2 %shard_map.120 = bf16[32,4096]{1,0:T(8,128)(2,1)S(1)} custom-call(f32[512,1024]{1,0:T(8,128)S(1)} %copy-done.1, f32[512,1]{1,0:T(8,128)S(1)} %copy.27.r_ref, f32[1,1024]{1,0:T(1,128)S(1)} %bitcast.9, bf16[1024,4096]{1,0:T(8,128)(2,1)} %w_hbm.1), custom_call_target="tpu_custom_call" | custom-call | tf_op jit(solution)/shard_map/pallas_call | solution.py:233
  193.9 0.7 copy.31
  (18 shorter events, 0.1 us)
Async XLA Ops:
  6.5 56.3 %all-gather.2.cloned.1.call-start = ((), (), s32[]{:S(2)}) async-start(), calls=%async_computation | async-start | bytes 4456448 | tf_op jit(solution)/shard_map/all_gather | solution.py:273
  85.4 6.5 %copy-start.6 = (bf16[512,2192]{1,0:T(8,128)(2,1)}, bf16[512,2192]{1,0:T(8,128)(2,1)S(1)}, u32[]{:S(2)}) copy-start(bf16[512,2192]{1,0:T(8,128)(2,1)S(1)} %get-tuple-element.22) | copy-start | bytes 6733828
  85.4 4.7 %collective-permute-start = (bf16[3,1152]{1,0:T(4,128)(2,1)S(1)}, bf16[3,1152]{1,0:T(4,128)(2,1)S(1)}, u32[]{:S(2)}, u32[]{:S(2)}) collective-permute-start(bf16[3,1152]{1,0:T(4,128)(2,1)S(1)} %slice.61), channel_id=1, source_target_pairs={{0,16},{1,17},{2,18},{3,19},{4,20},{5,21},{6,22},{7,23},{8,24},{9,... | collective-permute-start | bytes 20744 | tf_op jit(solution)/shard_map/ppermute | solution.py:26
  89.1 6.0 %copy-start.9 = (f32[16]{0:T(128)S(1)}, f32[16]{0:T(128)}, u32[]{:S(2)}) copy-start(f32[16]{0:T(128)} %param.19) | copy-start | bytes 196
  89.2 6.1 %copy-start.7 = (f32[16]{0:T(128)S(1)}, f32[16]{0:T(128)}, u32[]{:S(2)}) copy-start(f32[16]{0:T(128)} %param.20) | copy-start | bytes 196
  91.9 1.0 copy-start.5
  92.9 1.4 collective-permute-start.1
  94.5 8.4 %collective-permute-start.2 = (bf16[512,256]{1,0:T(8,128)(2,1)S(1)}, bf16[512,256]{1,0:T(8,128)(2,1)S(1)}, u32[]{:S(2)}, u32[]{:S(2)}) collective-permute-start(bf16[512,256]{1,0:T(8,128)(2,1)S(1)} %maximum_select_fusion.1), channel_id=1, source_target_pairs={{0,2},{1,3},{2,0},{3,1},{4,6},{5,7},{6,4},{7,5},{8,10},{9,11},{10,... | collective-permute-start | bytes 786440 | tf_op jit(solution)/shard_map/ppermute | solution.py:30
  97.9 17.9 %copy-start.8 = (f32[16]{0:T(128)S(1)}, f32[16]{0:T(128)}, u32[]{:S(2)}) copy-start(f32[16]{0:T(128)} %param.21) | copy-start | bytes 196
  110.1 1.4 copy-start.2
  111.6 14.9 %collective-permute-start.3 = (bf16[256,1024]{1,0:T(8,128)(2,1)S(1)}, bf16[256,1024]{1,0:T(8,128)(2,1)S(1)}, u32[]{:S(2)}, u32[]{:S(2)}) collective-permute-start(bf16[256,1024]{1,0:T(8,128)(2,1)S(1)} %convert_element_type.31), channel_id=1, source_target_pairs={{0,16},{1,17},{2,18},{3,19},{4,20},{5,21},{6,22},{7,23},{8,24},{9,... | collective-permute-start | bytes 1572872 | tf_op jit(solution)/shard_map/ppermute | solution.py:26
  116.0 10.5 %copy-start.3 = (f32[512,1024]{1,0:T(8,128)S(1)}, f32[512,1024]{1,0:T(8,128)}, u32[]{:S(2)}) copy-start(f32[512,1024]{1,0:T(8,128)} %copy-done.2) | copy-start | bytes 6291460
  126.4 9.7 %copy-start.4 = (f32[1024]{0:T(1024)S(1)}, f32[1024]{0:T(1024)}, u32[]{:S(2)}) copy-start(f32[1024]{0:T(1024)} %param.22) | copy-start | bytes 12292
  129.6 1.4 copy-start
  131.1 1.2 collective-permute-start.4
  132.3 3.6 %collective-permute-start.5 = (f32[512]{0:T(512)S(1)}, f32[512]{0:T(512)S(1)}, u32[]{:S(2)}, u32[]{:S(2)}) collective-permute-start(f32[512]{0:T(512)S(1)} %add.68), channel_id=1, source_target_pairs={{0,2},{1,3},{2,0},{3,1},{4,6},{5,7},{6,4},{7,5},{8,10},{9,11},{10,... | collective-permute-start | bytes 6152 | tf_op jit(solution)/shard_map/ppermute | solution.py:30
  136.1 1.6 copy-start.1
Sparse Core Ops, SparseCore 0:
  9.5 53.2 all-gather.1
